TPU v7x, 32 devices: a whole 2x2x4 slice. The times are simulated.
32 devices in a mesh: section: 4 (over x, core), fsdp: 2 (over y), batch: 4 (over z).
Axes of the slice: x: 2, y: 2, z: 4, core: 2. Of those that a mesh axis runs over, the one named last changes fastest.
Arguments:
- frames: bfloat16 [4, 8, 48, 1536], P(None, ('fsdp', 'batch')), may hold values from -6 to 6
- cotangent: bfloat16 [4, 8, 48, 1536], P(None, ('fsdp', 'batch')), may hold values from -6 to 6
- lengths: int32 [4, 8], P(None, ('fsdp', 'batch')), may hold values from 24 to 48
- w_in: bfloat16 [4, 1536, 3072], P('section', 'fsdp'), may hold values from -0.15625 to 0.15625
- w_out: bfloat16 [4, 1536, 1536], P('section', 'fsdp'), may hold values from -0.15625 to 0.15625
- gain_pre: float32 [4, 1536], P('section'), may hold values from 0.5 to 1.5
- gain_mid: float32 [4, 1536], P('section'), may hold values from 0.5 to 1.5
- w_depth: float32 [4, 31, 1536], P('section'), may hold values from -2 to 2
Outputs:
- input_grads: bfloat16 [4, 4, 8, 48, 1536], P('section', None, ('fsdp', 'batch'))
- grad_w_in: float32 [4, 1536, 3072], P('section', 'fsdp')
- grad_w_out: float32 [4, 1536, 1536], P('section', 'fsdp')
- grad_gain_pre: float32 [4, 1536], P('section')
- grad_gain_mid: float32 [4, 1536], P('section')
- grad_depth: float32 [4, 31, 1536], P('section')
Inputs may be any that keep to these rules, and one draw needn't show every extreme that they name: `lengths`: frames at or after an utterance's length are padding.
All inputs are finite; a program needn't handle non-finite values.
Results may differ from a plain program's by a relative error of at most 0.03.
Values may be sent and summed in bfloat16 or wider, within the bound.
A program may use at most 128 MiB of HBM per device.

v0:
```python
import math

import jax
import jax.numpy as jnp
from jax import lax
from jax.sharding import PartitionSpec as P

epsilon = 1e-05


def from_behind(x, axis, by):
    peers = lax.axis_size(axis)
    pairs = [(i, i + by) for i in range(peers) if 0 <= i + by < peers]
    return lax.ppermute(x, axis, pairs)


def layer_norm(values):
    mean_value = jnp.mean(values, axis=-1, keepdims=True)
    centred = values - mean_value
    inv_scale = lax.rsqrt(jnp.mean(centred * centred, axis=-1, keepdims=True) + epsilon)
    return (centred * inv_scale, inv_scale)


def norm_grad(upstream, normed, inv_scale):
    return (
        upstream
        - jnp.mean(upstream, axis=-1, keepdims=True)
        - normed * jnp.mean(upstream * normed, axis=-1, keepdims=True)
    ) * inv_scale


def project(left, right):
    batch_rows, length, inner = left.shape
    flat = jnp.dot(
        left.reshape(batch_rows * length, inner), right, preferred_element_type=jnp.float32
    )
    return flat.reshape(batch_rows, length, right.shape[1])


def project_back(left, right):
    batch_rows, length, inner = left.shape
    flat = lax.dot_general(
        left.reshape(batch_rows * length, inner),
        right,
        (((1,), (1,)), ((), ())),
        preferred_element_type=jnp.float32,
    )
    return flat.reshape(batch_rows, length, right.shape[0])


def depthwise(values, taps):
    kernel = taps.shape[0]
    half = kernel // 2
    length = values.shape[1]
    padded = jnp.pad(values, ((0, 0), (half, half), (0, 0)))
    total = padded[:, 0:length, :] * taps[0]
    for offset in range(1, kernel):
        total = total + padded[:, offset : offset + length, :] * taps[offset]
    return total


def section_forward(frames, w_in, w_out, gain_a, gain_b, taps, padding):
    model_width = frames.shape[-1]
    source = frames.astype(jnp.float32)
    normed_in, inv_in = layer_norm(source)
    projected = (normed_in * gain_a).astype(jnp.bfloat16)
    both = project(projected, w_in)
    glu_value = both[..., :model_width]
    glu_gate = jax.nn.sigmoid(both[..., model_width:])
    gated = glu_value * glu_gate * padding
    conv_out = depthwise(gated, taps)
    normed_mid, inv_mid = layer_norm(conv_out)
    scaled_mid = normed_mid * gain_b
    swished = (scaled_mid * jax.nn.sigmoid(scaled_mid)).astype(jnp.bfloat16)
    result = (source + project(swished, w_out)).astype(jnp.bfloat16)
    return (
        result,
        (
            normed_in,
            inv_in,
            projected,
            glu_value,
            glu_gate,
            gated,
            normed_mid,
            inv_mid,
            scaled_mid,
            swished,
        ),
    )


def section_backward(upstream, w_in, w_out, gain_a, gain_b, taps, padding, saved):
    (
        normed_in,
        inv_in,
        projected,
        glu_value,
        glu_gate,
        gated,
        normed_mid,
        inv_mid,
        scaled_mid,
        swished,
    ) = saved
    kernel = taps.shape[0]
    half = kernel // 2
    length = upstream.shape[1]
    swish_grad = project_back(upstream, w_out)
    sigmoid_mid = jax.nn.sigmoid(scaled_mid)
    scaled_grad = swish_grad * (sigmoid_mid + scaled_mid * sigmoid_mid * (1.0 - sigmoid_mid))
    gain_b_grad = jnp.sum(scaled_grad * normed_mid, axis=(0, 1))
    conv_grad = norm_grad(scaled_grad * gain_b, normed_mid, inv_mid)
    padded_in = jnp.pad(gated, ((0, 0), (half, half), (0, 0)))
    taps_grad = jnp.stack(
        [
            jnp.sum(conv_grad * padded_in[:, offset : offset + length, :], axis=(0, 1))
            for offset in range(kernel)
        ]
    )
    padded_grad = jnp.pad(conv_grad, ((0, 0), (half, half), (0, 0)))
    gated_grad = padded_grad[:, 2 * half : 2 * half + length, :] * taps[0]
    for offset in range(1, kernel):
        gated_grad = (
            gated_grad
            + padded_grad[:, 2 * half - offset : 2 * half - offset + length, :] * taps[offset]
        )
    gated_grad = gated_grad * padding
    value_grad = gated_grad * glu_gate
    gate_grad = gated_grad * glu_value * glu_gate * (1.0 - glu_gate)
    proj_grad = jnp.concatenate([value_grad, gate_grad], axis=-1).astype(jnp.bfloat16)
    input_side = project_back(proj_grad, w_in)
    gain_a_grad = jnp.sum(input_side * normed_in, axis=(0, 1))
    input_grad = (
        upstream.astype(jnp.float32) + norm_grad(input_side * gain_a, normed_in, inv_in)
    ).astype(jnp.bfloat16)
    return (input_grad, proj_grad, (gain_a_grad, gain_b_grad, taps_grad))


def saved_zeros(micro_count, frames_len, model_width):
    wide = (micro_count, 1, frames_len, model_width)
    narrow = (micro_count, 1, frames_len, 1)
    return (
        jnp.zeros(wide, jnp.float32),
        jnp.zeros(narrow, jnp.float32),
        jnp.zeros(wide, jnp.bfloat16),
        jnp.zeros(wide, jnp.float32),
        jnp.zeros(wide, jnp.float32),
        jnp.zeros(wide, jnp.float32),
        jnp.zeros(wide, jnp.float32),
        jnp.zeros(narrow, jnp.float32),
        jnp.zeros(wide, jnp.float32),
        jnp.zeros(wide, jnp.bfloat16),
    )


def put_slot(buffers, values, micro_slot):
    return jax.tree.map(
        lambda buffer, value: lax.dynamic_update_index_in_dim(buffer, value, micro_slot, 0),
        buffers,
        values,
    )


def take_slot(buffers, micro_slot):
    return jax.tree.map(
        lambda buffer: lax.dynamic_index_in_dim(buffer, micro_slot, 0, keepdims=False), buffers
    )


def local(frames, cotangent, lengths, w_in, w_out, gain_pre, gain_mid, w_depth):
    section_count = lax.axis_size("section")
    section_index = lax.axis_index("section")
    micro_count = frames.shape[0]
    frames_len = frames.shape[2]
    model_width = frames.shape[3]
    moments = micro_count + section_count - 1
    scale = 1.0 / math.sqrt(
        micro_count * frames_len * lax.axis_size("fsdp") * lax.axis_size("batch")
    )
    w_in_full, w_out_full = (
        lax.all_gather(w_in[0], "fsdp", axis=0, tiled=True),
        lax.all_gather(w_out[0], "fsdp", axis=0, tiled=True),
    )
    gain_a = gain_pre[0]
    gain_b = gain_mid[0]
    taps = w_depth[0]
    positions = jnp.arange(frames_len, dtype=jnp.int32)

    def frame_padding(micro_slot):
        return (positions < lengths[micro_slot, 0]).astype(jnp.float32).reshape(1, frames_len, 1)

    stored = saved_zeros(micro_count, frames_len, model_width)
    blank = jnp.zeros((1, frames_len, model_width), jnp.bfloat16)
    outgoing = blank
    for moment in range(moments):
        if moment > 0:
            incoming = from_behind(outgoing, "section", 1)
        else:
            incoming = blank
        if moment < micro_count:
            section_input = jnp.where(section_index == 0, frames[moment], incoming)
        else:
            section_input = incoming
        micro_index = moment - section_index
        active = (micro_index >= 0) & (micro_index < micro_count)
        micro_slot = jnp.clip(micro_index, 0, micro_count - 1)

        def advance(operands, micro_slot=micro_slot):
            current, buffers = operands
            result, saved = section_forward(
                current, w_in_full, w_out_full, gain_a, gain_b, taps, frame_padding(micro_slot)
            )
            return (result, put_slot(buffers, saved, micro_slot))

        def bypass(operands):
            return (jnp.zeros_like(operands[0]), operands[1])

        outgoing, stored = lax.cond(active, advance, bypass, (section_input, stored))
    row_buffers = (
        jnp.zeros((micro_count, frames_len, model_width), jnp.bfloat16),
        jnp.zeros((micro_count, frames_len, 2 * model_width), jnp.bfloat16),
        jnp.zeros((micro_count, frames_len, model_width), jnp.bfloat16),
        jnp.zeros((micro_count, frames_len, model_width), jnp.bfloat16),
        jnp.zeros((micro_count, frames_len, model_width), jnp.bfloat16),
    )
    small_sums = (
        jnp.zeros((model_width,), jnp.float32),
        jnp.zeros((model_width,), jnp.float32),
        jnp.zeros(taps.shape, jnp.float32),
    )
    returning = blank
    for moment in range(moments):
        if moment > 0:
            incoming = from_behind(returning, "section", -1)
        else:
            incoming = blank
        if moment < micro_count:
            upstream = jnp.where(section_index == section_count - 1, cotangent[moment], incoming)
        else:
            upstream = incoming
        micro_index = moment - (section_count - 1 - section_index)
        active = (micro_index >= 0) & (micro_index < micro_count)
        micro_slot = jnp.clip(micro_index, 0, micro_count - 1)

        def retreat(operands, micro_slot=micro_slot):
            current, buffers, totals = operands
            padding = frame_padding(micro_slot)
            saved = take_slot(stored, micro_slot)
            input_grad, proj_grad, minor_grads = section_backward(
                current, w_in_full, w_out_full, gain_a, gain_b, taps, padding, saved
            )
            row_values = (saved[2][0], proj_grad[0], saved[9][0], current[0], input_grad[0])
            buffers = put_slot(buffers, row_values, micro_slot)
            totals = tuple((total + extra for total, extra in zip(totals, minor_grads)))
            return (input_grad, buffers, totals)

        def hold(operands):
            return (jnp.zeros_like(operands[0]), operands[1], operands[2])

        returning, row_buffers, small_sums = lax.cond(
            active, retreat, hold, (upstream, row_buffers, small_sums)
        )
    total_rows = micro_count * frames_len
    proj_rows = row_buffers[0].reshape(total_rows, model_width)
    grad_rows = row_buffers[1].reshape(total_rows, 2 * model_width)
    swish_rows = row_buffers[2].reshape(total_rows, model_width)
    upstream_rows = row_buffers[3].reshape(total_rows, model_width)
    term_in = lax.dot_general(
        proj_rows, grad_rows, (((0,), (0,)), ((), ())), preferred_element_type=jnp.float32
    )
    term_out = lax.dot_general(
        swish_rows, upstream_rows, (((0,), (0,)), ((), ())), preferred_element_type=jnp.float32
    )
    rounded_in = lax.optimization_barrier(term_in.astype(jnp.bfloat16)).astype(jnp.float32)
    rounded_out = lax.optimization_barrier(term_out.astype(jnp.bfloat16)).astype(jnp.float32)
    shares = (
        lax.psum_scatter(
            rounded_in.astype(jnp.bfloat16), "fsdp", scatter_dimension=0, tiled=True
        ).astype(jnp.float32),
        lax.psum_scatter(
            rounded_out.astype(jnp.bfloat16), "fsdp", scatter_dimension=0, tiled=True
        ).astype(jnp.float32),
    )
    grad_in, grad_out = (
        lax.psum(shares[0].astype(jnp.bfloat16), "batch").astype(jnp.float32),
        lax.psum(shares[1].astype(jnp.bfloat16), "batch").astype(jnp.float32),
    )
    small_total = lax.psum((small_sums[0], small_sums[1], small_sums[2]), ("fsdp", "batch"))
    input_grads = row_buffers[4].reshape(1, micro_count, 1, frames_len, model_width)
    return (
        input_grads,
        (scale * grad_in)[None],
        (scale * grad_out)[None],
        (scale * small_total[0])[None],
        (scale * small_total[1])[None],
        (scale * small_total[2])[None],
    )


def solution(mesh):
    in_specs = (
        P(None, ("fsdp", "batch"), None, None),
        P(None, ("fsdp", "batch"), None, None),
        P(None, ("fsdp", "batch")),
        P("section", "fsdp", None),
        P("section", "fsdp", None),
        P("section", None),
        P("section", None),
        P("section", None, None),
    )
    out_specs = (
        P("section", None, ("fsdp", "batch"), None, None),
        P("section", "fsdp", None),
        P("section", "fsdp", None),
        P("section", None),
        P("section", None),
        P("section", None, None),
    )
    return jax.shard_map(local, mesh=mesh, in_specs=in_specs, out_specs=out_specs, check_vma=False)
```

profile of v0, /device:TPU:0, one launch (start us, length us, event | category | flops | bytes accessed | tf_op | source)
XLA Modules:
  0.0 1142.1 jit_solution(12173441752658840537)
XLA Ops:
  8.9 66.1 %all-gather.5.cloned.1.call-done = bf16[1,1536,1536]{2,1,0:T(8,128)(2,1)} async-done(((bf16[1,768,1536]{2,1,0:T(8,128)(2,1)}), bf16[1,1536,1536]{2,1,0:T(8,128)(2,1)}) %all-gather.5.cloned.1.call-update) | async-done | bytes 4718608 | tf_op jit(solution)/shard_map/all_gather | solution.py:183
  74.9 119.6 %all-gather.7.cloned.1.call-done = bf16[1,1536,3072]{2,1,0:T(8,128)(2,1)} async-done(((bf16[1,768,3072]{2,1,0:T(8,128)(2,1)}), bf16[1,1536,3072]{2,1,0:T(8,128)(2,1)}) %all-gather.7.cloned.1.call-update) | async-done | bytes 9437200 | tf_op jit(solution)/shard_map/all_gather | solution.py:182
  195.1 25.9 %conditional.14 = (bf16[1,48,1536]{2,1,0:T(8,128)(2,1)}, f32[4,1,48,1536]{3,2,1,0:T(8,128)}, f32[4,1,48,1]{2,3,1,0:T(1,128)}, bf16[4,1,48,1536]{3,2,1,0:T(8,128)...) conditional(s32[]{:T(128)} %convert_element_type.332, ...), branch_computations={%region_0.1_spmd, %region_1.6_spmd} | conditional | flops 688103936 | bytes 49525620 | solution.py:219
  195.6 5.5 convolution_bitcast_fusion
  224.1 18.9 %conditional.15 = (bf16[1,48,1536]{2,1,0:T(8,128)(2,1)}, f32[4,1,48,1536]{3,2,1,0:T(8,128)}, f32[4,1,48,1]{2,3,1,0:T(1,128)}, bf16[4,1,48,1536]{3,2,1,0:T(8,128)...) conditional(s32[]{:T(128)} %convert_element_type.331, ...), branch_computations={%region_6.7_spmd, %region_7.12_spmd} | conditional | flops 687735232 | bytes 22092980 | solution.py:219
  226.1 5.5 convolution_bitcast_fusion.2
  247.1 18.5 %conditional.16 = (bf16[1,48,1536]{2,1,0:T(8,128)(2,1)}, f32[4,1,48,1536]{3,2,1,0:T(8,128)}, f32[4,1,48,1]{2,3,1,0:T(1,128)}, bf16[4,1,48,1536]{3,2,1,0:T(8,128)...) conditional(s32[]{:T(128)} %convert_element_type.330, ...), branch_computations={%region_12.13_spmd, %region_13.18_spmd} | conditional | flops 687735232 | bytes 21503128 | solution.py:219
  248.6 5.5 convolution_bitcast_fusion.4
  269.8 17.1 %conditional.17 = (bf16[1,48,1536]{2,1,0:T(8,128)(2,1)}, f32[4,1,48,1536]{3,2,1,0:T(8,128)}, f32[4,1,48,1]{2,3,1,0:T(1,128)}, bf16[4,1,48,1536]{3,2,1,0:T(8,128)...) conditional(s32[]{:T(128)} %convert_element_type.329, ...), branch_computations={%region_18.19_spmd, %region_19.24_spmd} | conditional | flops 687735232 | bytes 21503220 | solution.py:219
  271.2 5.5 convolution_bitcast_fusion.6
  286.9 5.5 collective-permute-start.3
  294.6 20.9 %collective-permute-start.4 = (bf16[1,48,1536]{2,1,0:T(8,128)(2,1)}, bf16[1,48,1536]{2,1,0:T(8,128)(2,1)S(1)}, u32[]{:S(2)}, u32[]{:S(2)}) collective-permute-start(bf16[1,48,1536]{2,1,0:T(8,128)(2,1)} %get-tuple-element.1558), channel_id=1, source_target_pairs={{0,8},{8,16},{16,24},{1,9},{9,17},{17,25},{2,10},{10,18},{18,26},{... | collective-permute-start | bytes 442376 | tf_op jit(solution)/shard_map/ppermute | solution.py:14
  317.4 5.4 collective-permute-start.5
  330.7 20.5 %collective-permute-done.6 = bf16[1,48,1536]{2,1,0:T(8,128)(2,1)S(1)} collective-permute-done((bf16[1,48,1536]{2,1,0:T(8,128)(2,1)S(1)}, bf16[1,48,1536]{2,1,0:T(8,128)(2,1)S(1)}, u32[]{:S(2)}, u32[]{:S(2)}) %collective-permute-start.6) | collective-permute-done | bytes 147488 | tf_op jit(solution)/shard_map/ppermute | solution.py:14
  353.9 6.0 collective-permute-done.7
  361.3 5.8 collective-permute-start.8
  367.1 121.5 %collective-permute-done.8 = bf16[1,48,1536]{2,1,0:T(8,128)(2,1)S(1)} collective-permute-done((bf16[1,48,1536]{2,1,0:T(8,128)(2,1)}, bf16[1,48,1536]{2,1,0:T(8,128)(2,1)S(1)}, u32[]{:S(2)}, u32[]{:S(2)}) %collective-permute-start.8) | collective-permute-done | bytes 147488 | tf_op jit(solution)/shard_map/ppermute | solution.py:14
  489.0 39.9 %conditional.24 = (bf16[1,48,1536]{2,1,0:T(8,128)(2,1)}, bf16[4,48,1536]{2,1,0:T(8,128)(2,1)}, bf16[4,48,3072]{2,1,0:T(8,128)(2,1)}, bf16[4,48,1536]{2,1,0:T(8,1...) conditional(s32[]{:T(128)} %convert_element_type.322, ...), branch_computations={%region_159.160_spmd, %region_160.198_spmd} | conditional | flops 692822144 | bytes 26455680 | solution.py:261
  518.6 6.8 fusion.1096
  536.2 24.4 %conditional.25 = (bf16[1,48,1536]{2,1,0:T(8,128)(2,1)S(1)}, bf16[4,48,1536]{2,1,0:T(8,128)(2,1)}, bf16[4,48,3072]{2,1,0:T(8,128)(2,1)}, bf16[4,48,1536]{2,1,0:T...) conditional(s32[]{:T(128)} %convert_element_type.321, ...), branch_computations={%region_198.199_spmd, %region_199.237_spmd} | conditional | flops 692748416 | bytes 27118580 | solution.py:261
  550.3 6.8 fusion.1244
  567.7 24.5 %conditional.26 = (bf16[1,48,1536]{2,1,0:T(8,128)(2,1)S(1)}, bf16[4,48,1536]{2,1,0:T(8,128)(2,1)}, bf16[4,48,3072]{2,1,0:T(8,128)(2,1)}, bf16[4,48,1536]{2,1,0:T...) conditional(s32[]{:T(128)} %convert_element_type.320, ...), branch_computations={%region_237.238_spmd, %region_238.276_spmd} | conditional | flops 692748416 | bytes 27118580 | solution.py:261
  581.9 6.8 fusion.1392
  598.6 24.5 %conditional.27 = (bf16[4,48,1536]{2,1,0:T(8,128)(2,1)}, bf16[4,48,3072]{2,1,0:T(8,128)(2,1)}, bf16[4,48,1536]{2,1,0:T(8,128)(2,1)}, bf16[4,48,1536]{2,1,0:T(8,1...) conditional(s32[]{:T(128)} %convert_element_type.319, ...), branch_computations={%region_276.277_spmd, %region_277.315_spmd} | conditional | flops 692748416 | bytes 25938872 | solution.py:261
  608.5 6.8 fusion.1538
  628.2 8.0 bitcast_convert_fusion
  636.8 50.5 %reduce-scatter.5.cloned.1.call-done = bf16[768,1536]{1,0:T(8,128)(2,1)} async-done(((bf16[1536,1536]{1,0:T(8,128)(2,1)}), bf16[768,1536]{1,0:T(8,128)(2,1)}) %reduce-scatter.5.cloned.1.call-update) | async-done | bytes 2359312 | tf_op jit(solution)/shard_map/reduce_scatter | solution.py:281
  687.3 113.4 %reduce-scatter.3.cloned.1.call-done = bf16[768,3072]{1,0:T(8,128)(2,1)} async-done(((bf16[1536,3072]{1,0:T(8,128)(2,1)}), bf16[768,3072]{1,0:T(8,128)(2,1)}) %reduce-scatter.3.cloned.1.call-update) | async-done | bytes 4718608 | tf_op jit(solution)/shard_map/reduce_scatter | solution.py:278
  800.8 36.5 %all-reduce.21 = (f32[1536]{0:T(1024)S(1)}, f32[1536]{0:T(1024)S(1)}) all-reduce(f32[1536]{0:T(1024)S(1)} %get-tuple-element.1639, f32[1536]{0:T(1024)S(1)} %get-tuple-element.1640), channel_id=1, replica_groups=mesh['section'=4,'fsdp'=2,'batch'=4] {'fsdp','batch'}, use_global_device_ids=true, to_apply=%region_319.320 | all-reduce | flops 3072 | bytes 24576 | tf_op jit(solution)/shard_map/psum | solution.py:289
  838.5 35.9 %all-reduce.26.cloned.1.call-done = f32[31,1536]{1,0:T(8,128)} async-done(((f32[31,1536]{1,0:T(8,128)}), f32[31,1536]{1,0:T(8,128)}) %all-reduce.26.cloned.1.call-update) | async-done | bytes 190480 | tf_op jit(solution)/shard_map/psum | solution.py:289
  876.1 248.3 %all-reduce.28.cloned.1.call-done = (bf16[768,3072]{1,0:T(8,128)(2,1)}, bf16[768,1536]{1,0:T(8,128)(2,1)}) async-done(((bf16[768,3072]{1,0:T(8,128)(2,1)}, bf16[768,1536]{1,0:T(8,128)(2,1)}), (bf16[768,3072]{1,0:T(8,128)(2,1)}, bf16[768,1536]{1,0:T(8,128)(2,1)})) %all-reduce.28.cloned.1.call-update) | async-done | bytes 7077904 | tf_op jit(solution)/shard_map/psum | solution.py:286
  1124.4 7.5 multiply_bitcast_fusion
  (437 shorter events, 211.7 us)
Async XLA Ops:
  7.2 67.8 %all-gather.5.cloned.1.call-start = ((), (), s32[]{:S(2)}) async-start(), calls=%async_computation.5 | async-start | bytes 7077888 | tf_op jit(solution)/shard_map/all_gather | solution.py:183
  7.9 187.2 %copy-start.6 = (f32[1,1536]{1,0:T(1,128)S(1)}, f32[1,1536]{1,0:T(1,128)}, u32[]{:S(2)}) copy-start(f32[1,1536]{1,0:T(1,128)} %param.41) | copy-start | bytes 18436
  7.9 187.2 %copy-start.7 = (f32[1,1536]{1,0:T(1,128)S(1)}, f32[1,1536]{1,0:T(1,128)}, u32[]{:S(2)}) copy-start(f32[1,1536]{1,0:T(1,128)} %param.42) | copy-start | bytes 18436
  7.9 187.2 %copy-start.12 = (bf16[4,1,48,1536]{3,2,1,0:T(8,128)(2,1)S(1)}, bf16[4,1,48,1536]{3,2,1,0:T(8,128)(2,1)}, u32[]{:S(2)}) copy-start(bf16[4,1,48,1536]{3,2,1,0:T(8,128)(2,1)} %param.36) | copy-start | bytes 1769476
  7.9 186.6 %all-gather.7.cloned.1.call-start = ((), (), s32[]{:S(2)}) async-start(), calls=%async_computation.6 | async-start | bytes 14155776 | tf_op jit(solution)/shard_map/all_gather | solution.py:182
  8.7 678.6 %reduce-scatter.5.cloned.1.call-start = ((), (), s32[]{:S(2)}) async-start(), calls=%async_computation.3 | async-start | bytes 7077888 | tf_op jit(solution)/shard_map/reduce_scatter | solution.py:281
  195.6 5.5 copy-start.22
  195.6 6.1 copy-start.30
  208.2 5.8 copy-start
  216.3 4.8 copy-start.17
  221.1 2.5 collective-permute-start
  243.0 3.6 collective-permute-start.1
  265.5 4.3 collective-permute-start.2
  271.2 5.5 copy-start.23
  286.9 6.7 collective-permute-start.3
  294.6 22.1 %collective-permute-start.4 = (bf16[1,48,1536]{2,1,0:T(8,128)(2,1)}, bf16[1,48,1536]{2,1,0:T(8,128)(2,1)S(1)}, u32[]{:S(2)}, u32[]{:S(2)}) collective-permute-start(bf16[1,48,1536]{2,1,0:T(8,128)(2,1)} %get-tuple-element.1558), channel_id=1, source_target_pairs={{0,8},{8,16},{16,24},{1,9},{9,17},{17,25},{2,10},{10,18},{18,26},{... | collective-permute-start | bytes 442376 | tf_op jit(solution)/shard_map/ppermute | solution.py:14
  317.4 6.6 collective-permute-start.5
  324.0 27.7 %copy-start.18 = (f32[4,1,48,1]{2,3,1,0:T(1,128)}, f32[4,1,48,1]{2,3,1,0:T(1,128)S(1)}, u32[]{:S(2)}) copy-start(f32[4,1,48,1]{2,3,1,0:T(1,128)S(1)} %get-tuple-element.2820) | copy-start | bytes 2308
  329.4 21.8 %collective-permute-start.6 = (bf16[1,48,1536]{2,1,0:T(8,128)(2,1)S(1)}, bf16[1,48,1536]{2,1,0:T(8,128)(2,1)S(1)}, u32[]{:S(2)}, u32[]{:S(2)}) collective-permute-start(bf16[1,48,1536]{2,1,0:T(8,128)(2,1)S(1)} %get-tuple-element.1588), channel_id=1, source_target_pairs={{8,0},{16,8},{24,16},{9,1},{17,9},{25,17},{10,2},{18,10},{26,18},{... | collective-permute-start | bytes 442376 | tf_op jit(solution)/shard_map/ppermute | solution.py:14
  352.6 7.3 collective-permute-start.7
  361.3 127.2 %collective-permute-start.8 = (bf16[1,48,1536]{2,1,0:T(8,128)(2,1)}, bf16[1,48,1536]{2,1,0:T(8,128)(2,1)S(1)}, u32[]{:S(2)}, u32[]{:S(2)}) collective-permute-start(bf16[1,48,1536]{2,1,0:T(8,128)(2,1)} %get-tuple-element.1606), channel_id=1, source_target_pairs={{8,0},{16,8},{24,16},{9,1},{17,9},{25,17},{10,2},{18,10},{26,18},{... | collective-permute-start | bytes 442376 | tf_op jit(solution)/shard_map/ppermute | solution.py:14
  518.6 6.8 copy-start.21
  528.9 6.6 collective-permute-start.9
  550.3 6.9 copy-start.11
  560.6 6.5 collective-permute-start.10
  581.8 6.9 copy-start.9
  592.2 6.4 collective-permute-start.11
  623.1 4.9 copy-start.4
  628.1 172.6 %reduce-scatter.3.cloned.1.call-start = ((), (), s32[]{:S(2)}) async-start(), calls=%async_computation.2 | async-start | bytes 14155776 | tf_op jit(solution)/shard_map/reduce_scatter | solution.py:278
  636.2 238.2 %all-reduce.26.cloned.1.call-start = ((), (), s32[]{:S(2)}) async-start(), calls=%async_computation.4 | async-start | bytes 393216 | tf_op jit(solution)/shard_map/psum | solution.py:289
  636.8 487.6 %all-reduce.28.cloned.1.call-start = ((), (), s32[]{:S(2)}) async-start(), calls=%async_computation.7 | async-start | bytes 14155776 | tf_op jit(solution)/shard_map/psum | solution.py:286
  1124.4 7.5 copy-start.5
  (11 other events, 27.6 us)
Sparse Core Ops, SparseCore 0:
  9.5 65.3 all-gather.4
  76.5 117.9 all-gather.6
  628.2 59.0 reduce-scatter.4
  690.2 110.5 reduce-scatter.2
  804.2 70.0 all-reduce.25
  876.7 247.6 all-reduce.27
where the time goes:
time: 1150 us; the launch traced here: 1140 us
  waiting for transfers between devices  806 us (70%)
  matrix products  94.2 us (8%)
  other arithmetic  71.9 us (6%)
  local copies, waits for them, and re-layouts  63.8 us (6%)
  starting transfers between devices  50.9 us (4%)
  blocking collectives  36.5 us (3%)
  between operations  14.9 us (1%)
    psum x1, waiting for transfers between devices, local(): lax.psum(shares[0].astype(jnp.bfloat16), 'batch').astype(jnp.float32)  248 us
    ppermute x12, waiting for transfers between devices, from_behind(): return lax.ppermute(x, axis, pairs)  171 us
    all_gather x1, waiting for transfers between devices, local(): lax.all_gather(w_in[0], 'fsdp', axis=0, tiled=True)  120 us
    reduce_scatter x1, waiting for transfers between devices, local(): lax.psum_scatter(rounded_in.astype(jnp.bfloat16), 'fsdp', scatter_dimensi...  113 us
    all_gather x1, waiting for transfers between devices, local(): lax.all_gather(w_out[0], 'fsdp', axis=0, tiled=True)  66.1 us
    ppermute x12, starting transfers between devices, from_behind(): return lax.ppermute(x, axis, pairs)  50.7 us
    reduce_scatter x1, waiting for transfers between devices, local(): lax.psum_scatter(rounded_out.astype(jnp.bfloat16), 'fsdp', scatter_dimens...  50.5 us
    dot_general x8, matrix products, project_back(): lax.dot_general(left.reshape(batch_rows * length, inner), right, (((1,),...  43.3 us
  transfers between devices with their start and end apart: 18, of which 18 were waited for; matrix products, arithmetic and copies ran while one was open for 1% of the time, Pallas kernels for 0%

commit v1 on v0

--- a/solution.py
+++ b/solution.py
@@ -1,11 +1,15 @@
+import functools
 import math
 
 import jax
 import jax.numpy as jnp
 from jax import lax
+from jax.experimental import pallas as pl
+from jax.experimental.pallas import tpu as pltpu
 from jax.sharding import PartitionSpec as P
 
 epsilon = 1e-05
+GROUP = 2
 
 
 def from_behind(x, axis, by):
@@ -298,6 +302,593 @@
     )
 
 
+TILE = 256
+LANES = 128
+EDGE = 16
+
+
+def pipeline_kernel(
+    dims,
+    frames,
+    cotangent,
+    pad,
+    w_in,
+    w_out,
+    gain_pre,
+    gain_mid,
+    taps,
+    ig,
+    total,
+    small_total,
+    win,
+    wout,
+    xin,
+    xout,
+    nin,
+    inv_in,
+    proj,
+    val,
+    gate,
+    gpad,
+    nmid,
+    inv_mid,
+    sw,
+    mid,
+    cpad,
+    tg,
+    lp,
+    ls,
+    right,
+    part,
+    arrived,
+    small,
+    small_y,
+    small_sum,
+    small_a,
+    small_b,
+    w_ys,
+    w_yr,
+    w_zs,
+    w_zr,
+    w_loc,
+    f_s,
+    f_r,
+    b_s,
+    b_r,
+    yp_s,
+    yp_r,
+    ysw_s,
+    ysw_r,
+    yu_s,
+    yu_r,
+    yg_s,
+    yg_r,
+    sy_s,
+    sy_r,
+    a_s,
+    a_r,
+    c_s,
+    c_r,
+    t_s,
+    t_r,
+):
+    steps, group, length, width, kernel = dims
+    rows = group * length
+    tiles = width // TILE
+    half = width // 2
+    f32, bf16 = jnp.float32, jnp.bfloat16
+    sections = lax.axis_size("section")
+    sec = lax.axis_index("section")
+    fs = lax.axis_index("fsdp")
+    ba = lax.axis_index("batch")
+    other = 1 - fs
+    mate = ba + 1 - 2 * lax.rem(ba, 2)
+    parity = lax.rem(ba, 2)
+    edge = (ba == 0) | (ba == 3)
+    inner = jnp.where(ba == 0, 1, 2)
+    outer = jnp.where(ba == 1, 0, 3)
+    opposite = 3 - ba
+
+    def remote(src, dst, send, recv, **where):
+        return pltpu.make_async_remote_copy(
+            src_ref=src,
+            dst_ref=dst,
+            send_sem=send,
+            recv_sem=recv,
+            device_id=where,
+            device_id_type=pl.DeviceIdType.MESH,
+        )
+
+    def tile(j, base=0):
+        return pl.ds(pl.multiple_of(base + j * TILE, TILE), TILE)
+
+    barrier = pltpu.get_barrier_semaphore()
+    for where in (
+        {"section": lax.rem(sec + 1, sections)},
+        {"section": lax.rem(sec + sections - 1, sections)},
+        {"fsdp": other},
+        {"batch": lax.rem(ba + 1, 4)},
+        {"batch": lax.rem(ba + 3, 4)},
+    ):
+        pl.semaphore_signal(barrier, inc=1, device_id=where, device_id_type=pl.DeviceIdType.MESH)
+    pl.semaphore_wait(barrier, 5)
+
+    pieces = []
+    in_rows, out_rows = half // 8, half // 4
+    for i in range(6):
+        if i < 4:
+            pieces.append((w_in, win, in_rows, (2 * i, 2 * i)))
+        else:
+            pieces.append((w_out, wout, out_rows, (2 * (i - 4), 2 * (i - 4))))
+
+    def span(size, first, which, owner=None):
+        begin = (first + which) * size
+        if owner is not None:
+            begin = owner * half + begin
+        return pl.ds(pl.multiple_of(begin, 16), size)
+
+    def over_y(i):
+        src, dst, size, (first, _) = pieces[i]
+        return remote(
+            src.at[span(size, first, parity)],
+            dst.at[span(size, first, parity, fs)],
+            w_ys.at[i],
+            w_yr.at[i],
+            fsdp=other,
+        )
+
+    def over_z(i):
+        _, dst, size, (first, _) = pieces[i]
+        block = dst.at[span(size, first, parity, other)]
+        return remote(block, block, w_zs.at[i], w_zr.at[i], batch=mate)
+
+    for i in range(6):
+        over_y(i).start()
+    own = pl.ds(pl.multiple_of(fs * half, 16), half)
+    own_in = pltpu.make_async_copy(w_in, win.at[own], w_loc.at[0])
+    own_out = pltpu.make_async_copy(w_out, wout.at[own], w_loc.at[1])
+    own_in.start()
+    own_out.start()
+
+    gpad[...] = jnp.zeros_like(gpad)
+    cpad[...] = jnp.zeros_like(cpad)
+    tg[...] = jnp.zeros_like(tg)
+    small[...] = jnp.zeros_like(small)
+
+    for i in range(6):
+        over_y(i).wait_recv()
+        over_z(i).start()
+    own_in.wait()
+    own_out.wait()
+    for i in range(6):
+        over_z(i).wait_recv()
+
+    mine = pl.ds(pl.multiple_of(fs * half, LANES), half)
+    theirs = pl.ds(pl.multiple_of(other * half, LANES), half)
+
+    def send_forward(s):
+        return remote(xout.at[s], xin.at[s], f_s.at[s], f_r.at[s], section=lax.rem(sec + 1, sections))
+
+    def send_backward(s):
+        return remote(
+            ig.at[s],
+            right.at[s, :, pl.ds(2 * width, width)],
+            b_s.at[s],
+            b_r.at[s],
+            section=lax.rem(sec + sections - 1, sections),
+        )
+
+    def send_proj(s):
+        return remote(proj.at[s, :, theirs], lp.at[steps + s], yp_s.at[s], yp_r.at[s], fsdp=other)
+
+    def send_sw(s):
+        return remote(sw.at[s, :, theirs], ls.at[steps + s], ysw_s.at[s], ysw_r.at[s], fsdp=other)
+
+    def send_up(s):
+        cols = pl.ds(2 * width, width)
+        return remote(
+            right.at[s, :, cols], right.at[steps + s, :, cols], yu_s.at[s], yu_r.at[s], fsdp=other
+        )
+
+    def send_grad(s):
+        cols = pl.ds(0, 2 * width)
+        return remote(
+            right.at[s, :, cols], right.at[steps + s, :, cols], yg_s.at[s], yg_r.at[s], fsdp=other
+        )
+
+    def norm_stats(values):
+        mean_value = jnp.sum(values, axis=-1, keepdims=True) * (1.0 / width)
+        centred = values - mean_value
+        inv = lax.rsqrt(jnp.sum(centred * centred, axis=-1, keepdims=True) * (1.0 / width) + epsilon)
+        return centred * inv, inv
+
+    def forward(s, carry):
+        @pl.when(sec == 0)
+        def _():
+            xin[s] = frames[s]
+
+        @pl.when(sec > 0)
+        def _():
+            send_forward(s).wait_recv()
+
+        normed, inv = norm_stats(xin[s].astype(f32))
+        nin[s] = normed
+        inv_in[s] = inv
+        proj[s] = (normed * gain_pre[...]).astype(bf16)
+        send_proj(s).start()
+        lp[s] = proj[s, :, mine]
+
+        def first(j, carry):
+            left = proj[s]
+            v = jnp.dot(left, win[:, tile(j)], preferred_element_type=f32)
+            g = jax.nn.sigmoid(
+                jnp.dot(left, win[:, tile(j, width)], preferred_element_type=f32)
+            )
+            val[s, :, tile(j)] = v
+            gate[s, :, tile(j)] = g
+            gated = v * g * pad[s]
+            for m in range(group):
+                gpad[s * group + m, EDGE : EDGE + length, tile(j)] = gated[
+                    m * length : (m + 1) * length
+                ]
+            for m in range(group):
+                for c in range(TILE // LANES):
+                    cols = pl.ds(pl.multiple_of(j * TILE + c * LANES, LANES), LANES)
+                    acc = jnp.zeros((length, LANES), f32)
+                    for b in range(8):
+                        rolled = gpad[s * group + m, b : b + length + 24, cols]
+                        for a in range(4):
+                            k = 8 * a + b - 1
+                            if 0 <= k < kernel:
+                                acc = acc + rolled[8 * a : 8 * a + length] * taps[k : k + 1, cols]
+                    mid[m * length : (m + 1) * length, cols] = acc
+            return carry
+
+        lax.fori_loop(0, tiles, first, 0)
+        normed2, inv2 = norm_stats(mid[...])
+        nmid[s] = normed2
+        inv_mid[s] = inv2
+        scaled = normed2 * gain_mid[...]
+        sw[s] = (scaled * jax.nn.sigmoid(scaled)).astype(bf16)
+        send_sw(s).start()
+        ls[s] = sw[s, :, mine]
+
+        @pl.when(sec < sections - 1)
+        def _():
+            def second(j, carry):
+                out = jnp.dot(sw[s], wout[:, tile(j)], preferred_element_type=f32)
+                xout[s, :, tile(j)] = (xin[s, :, tile(j)].astype(f32) + out).astype(bf16)
+                return carry
+
+            lax.fori_loop(0, tiles, second, 0)
+            send_forward(s).start()
+
+        return carry
+
+    lax.fori_loop(0, steps, forward, 0)
+
+    nt = (((1,), (1,)), ((), ()))
+
+    def backward(s, carry):
+        @pl.when(sec == sections - 1)
+        def _():
+            right[s, :, pl.ds(2 * width, width)] = cotangent[s]
+
+        @pl.when(sec < sections - 1)
+        def _():
+            send_backward(s).wait_recv()
+
+        send_up(s).start()
+        zero = jnp.zeros((rows, 1), f32)
+
+        def first(j, sums):
+            up = right[s, :, pl.ds(2 * width, width)]
+            sg = lax.dot_general(up, wout[tile(j), :], nt, preferred_element_type=f32)
+            nm = nmid[s, :, tile(j)]
+            gb = gain_mid[:, tile(j)]
+            scaled = nm * gb
+            sig = jax.nn.sigmoid(scaled)
+            scg = sg * (sig + scaled * sig * (1.0 - sig))
+            small[1:2, tile(j)] += jnp.sum(scg * nm, axis=0, keepdims=True)
+            z = scg * gb
+            mid[:, tile(j)] = z
+            return (
+                sums[0] + jnp.sum(z, axis=-1, keepdims=True),
+                sums[1] + jnp.sum(z * nm, axis=-1, keepdims=True),
+            )
+
+        s1, s2 = lax.fori_loop(0, tiles, first, (zero, zero))
+        s1 = s1 * (1.0 / width)
+        s2 = s2 * (1.0 / width)
+
+        def second(j, carry):
+            cols = pl.ds(pl.multiple_of(j * LANES, LANES), LANES)
+            gate_cols = pl.ds(pl.multiple_of(width + j * LANES, LANES), LANES)
+            cg_all = (mid[:, cols] - s1 - nmid[s, :, cols] * s2) * inv_mid[s]
+            for m in range(group):
+                span_m = slice(m * length, (m + 1) * length)
+                cg = cg_all[span_m]
+                cpad[m, EDGE : EDGE + length, :] = cg
+                for b in range(8):
+                    rolled = gpad[s * group + m, b : b + length + 24, cols]
+                    for a in range(4):
+                        k = 8 * a + b - 1
+                        if 0 <= k < kernel:
+                            term = cg * rolled[8 * a : 8 * a + length]
+                            tg[k, :, cols] += jnp.sum(term.reshape(length // 8, 8, LANES), axis=0)
+                acc = jnp.zeros((length, LANES), f32)
+                for b in range(8):
+                    rolled = cpad[m, b : b + length + 24, :]
+                    for a in range(4):
+                        k = kernel - 1 - (8 * a + b - 1)
+                        if 0 <= k < kernel:
+                            acc = acc + rolled[8 * a : 8 * a + length] * taps[k : k + 1, cols]
+                acc = acc * pad[s, span_m]
+                g = gate[s, span_m, cols]
+                vg = acc * g
+                right[s, span_m, cols] = vg.astype(bf16)
+                right[s, span_m, gate_cols] = (
+                    acc * val[s, span_m, cols] * g * (1.0 - g)
+                ).astype(bf16)
+            return carry
+
+        lax.fori_loop(0, width // LANES, second, 0)
+        send_grad(s).start()
+
+        def third(j, sums):
+            pg = right[s, :, pl.ds(0, 2 * width)]
+            ins = lax.dot_general(pg, win[tile(j), :], nt, preferred_element_type=f32)
+            nv = nin[s, :, tile(j)]
+            small[0:1, tile(j)] += jnp.sum(ins * nv, axis=0, keepdims=True)
+            z = ins * gain_pre[:, tile(j)]
+            mid[:, tile(j)] = z
+            return (
+                sums[0] + jnp.sum(z, axis=-1, keepdims=True),
+                sums[1] + jnp.sum(z * nv, axis=-1, keepdims=True),
+            )
+
+        m1, m2 = lax.fori_loop(0, tiles, third, (zero, zero))
+        m1 = m1 * (1.0 / width)
+        m2 = m2 * (1.0 / width)
+        up = right[s, :, pl.ds(2 * width, width)].astype(f32)
+        ig[s] = (up + (mid[...] - m1 - nin[s] * m2) * inv_in[s]).astype(bf16)
+
+        @pl.when(sec > 0)
+        def _():
+            send_backward(s).start()
+
+        return carry
+
+    lax.fori_loop(0, steps, backward, 0)
+
+    small[8 : 8 + kernel] = jnp.sum(tg[...], axis=1)
+    swap = remote(small, small_y, sy_s, sy_r, fsdp=other)
+    swap.start()
+
+    def arrivals(s, carry):
+        send_proj(s).wait_recv()
+        send_sw(s).wait_recv()
+        send_up(s).wait_recv()
+        send_grad(s).wait_recv()
+        return carry
+
+    lax.fori_loop(0, steps, arrivals, 0)
+    swap.wait_recv()
+    small_sum[...] = small[...] + small_y[...]
+
+    chunks = 3 * tiles
+
+    def chunk_to_inner(c):
+        return remote(
+            part.at[:, tile(c)], arrived.at[:, tile(c)], a_s.at[c], a_r.at[c], batch=inner
+        )
+
+    def chunk_across(c):
+        return remote(
+            part.at[:, tile(c)], total.at[:, tile(c)], c_s.at[c], c_r.at[c], batch=opposite
+        )
+
+    def chunk_to_outer(c):
+        return remote(
+            total.at[:, tile(c)], total.at[:, tile(c)], t_s.at[c], t_r.at[c], batch=outer
+        )
+
+    small_to_inner = remote(small_sum, small_a, a_s.at[chunks], a_r.at[chunks], batch=inner)
+    small_across = remote(small_sum, small_b, c_s.at[chunks], c_r.at[chunks], batch=opposite)
+    small_to_outer = remote(small_total, small_total, t_s.at[chunks], t_r.at[chunks], batch=outer)
+
+    tn = (((0,), (0,)), ((), ()))
+
+    def terms(left_ref, first_chunk, count):
+        def one(c, carry):
+            left = left_ref[...].reshape(2 * steps * rows, half)
+            block = right[:, :, tile(c)].reshape(2 * steps * rows, TILE)
+            part[:, tile(c)] = lax.dot_general(
+                left, block, tn, preferred_element_type=f32
+            ).astype(bf16)
+
+            @pl.when(edge)
+            def _():
+                chunk_to_inner(c).start()
+
+            return carry
+
+        lax.fori_loop(first_chunk, first_chunk + count, one, 0)
+
+    @pl.when(edge)
+    def _():
+        small_to_inner.start()
+
+    terms(lp, 0, 2 * tiles)
+    terms(ls, 2 * tiles, tiles)
+
+    @pl.when(jnp.logical_not(edge))
+    def _():
+        small_to_inner.wait_recv()
+        small_sum[...] = small_sum[...] + small_a[...]
+        small_across.start()
+
+        def finish(c):
+            chunk_across(c).wait_recv()
+            chunk_across(c).wait_send()
+            total[:, tile(c)] = (
+                part[:, tile(c)].astype(f32) + total[:, tile(c)].astype(f32)
+            ).astype(bf16)
+            chunk_to_outer(c).start()
+
+        def meet(c, carry):
+            chunk_to_inner(c).wait_recv()
+            part[:, tile(c)] = (
+                part[:, tile(c)].astype(f32) + arrived[:, tile(c)].astype(f32)
+            ).astype(bf16)
+            chunk_across(c).start()
+
+            @pl.when(c > 0)
+            def _():
+                finish(c - 1)
+
+            return carry
+
+        lax.fori_loop(0, chunks, meet, 0)
+        finish(chunks - 1)
+        small_across.wait_recv()
+        small_across.wait_send()
+        small_total[...] = small_sum[...] + small_b[...]
+        small_to_outer.start()
+
+        def sent(c, carry):
+            chunk_to_outer(c).wait_send()
+            return carry
+
+        lax.fori_loop(0, chunks, sent, 0)
+        small_to_outer.wait_send()
+
+    @pl.when(edge)
+    def _():
+        def done(c, carry):
+            chunk_to_inner(c).wait_send()
+            chunk_to_outer(c).wait_recv()
+            return carry
+
+        lax.fori_loop(0, chunks, done, 0)
+        small_to_inner.wait_send()
+        small_to_outer.wait_recv()
+
+    for i in range(6):
+        over_y(i).wait_send()
+        over_z(i).wait_send()
+    swap.wait_send()
+
+    def drained(s, carry):
+        send_proj(s).wait_send()
+        send_sw(s).wait_send()
+        send_up(s).wait_send()
+        send_grad(s).wait_send()
+
+        @pl.when(sec < sections - 1)
+        def _():
+            send_forward(s).wait_send()
+
+        @pl.when(sec > 0)
+        def _():
+            send_backward(s).wait_send()
+
+        return carry
+
+    lax.fori_loop(0, steps, drained, 0)
+
+
+def fused(frames, cotangent, lengths, w_in, w_out, gain_pre, gain_mid, w_depth):
+    micro_count, _, length, width = frames.shape
+    kernel = w_depth.shape[1]
+    group = GROUP
+    steps = micro_count // group
+    rows = group * length
+    half = w_in.shape[1]
+    scale = 1.0 / math.sqrt(micro_count * length * lax.axis_size("fsdp") * lax.axis_size("batch"))
+    positions = jnp.arange(length, dtype=jnp.int32)
+    pad = (positions[None, :] < lengths).astype(jnp.float32).reshape(steps, rows, 1)
+    f32, bf16 = jnp.float32, jnp.bfloat16
+    chunks = 3 * (width // TILE)
+    small_rows = 8 + -(-kernel // 8) * 8
+    vmem = pl.BlockSpec(memory_space=pltpu.VMEM)
+    hbm = pl.BlockSpec(memory_space=pl.ANY)
+
+    def buf(*shape, dtype=f32):
+        return pltpu.VMEM(shape, dtype)
+
+    def sem(*shape):
+        return pltpu.SemaphoreType.DMA(shape)
+
+    ig, total, small = pl.pallas_call(
+        functools.partial(pipeline_kernel, (steps, group, length, width, kernel)),
+        out_shape=(
+            jax.ShapeDtypeStruct((steps, rows, width), bf16),
+            jax.ShapeDtypeStruct((half, 3 * width), bf16),
+            jax.ShapeDtypeStruct((small_rows, width), f32),
+        ),
+        in_specs=[vmem, vmem, vmem, hbm, hbm, vmem, vmem, vmem],
+        out_specs=(vmem, vmem, vmem),
+        scratch_shapes=[
+            buf(width, 2 * width, dtype=bf16),
+            buf(width, width, dtype=bf16),
+            buf(steps, rows, width, dtype=bf16),
+            buf(steps, rows, width, dtype=bf16),
+            buf(steps, rows, width),
+            buf(steps, rows, 1),
+            buf(steps, rows, width, dtype=bf16),
+            buf(steps, rows, width),
+            buf(steps, rows, width),
+            buf(micro_count, length + 2 * EDGE, width),
+            buf(steps, rows, width),
+            buf(steps, rows, 1),
+            buf(steps, rows, width, dtype=bf16),
+            buf(rows, width),
+            buf(group, length + 2 * EDGE, LANES),
+            buf(kernel, 8, width),
+            buf(2 * steps, rows, half, dtype=bf16),
+            buf(2 * steps, rows, half, dtype=bf16),
+            buf(2 * steps, rows, 3 * width, dtype=bf16),
+            buf(half, 3 * width, dtype=bf16),
+            buf(half, 3 * width, dtype=bf16),
+            buf(small_rows, width),
+            buf(small_rows, width),
+            buf(small_rows, width),
+            buf(small_rows, width),
+            buf(small_rows, width),
+            sem(6),
+            sem(6),
+            sem(6),
+            sem(6),
+            sem(2),
+            *[sem(steps) for _ in range(12)],
+            pltpu.SemaphoreType.DMA,
+            pltpu.SemaphoreType.DMA,
+            *[sem(chunks + 1) for _ in range(6)],
+        ],
+        compiler_params=pltpu.CompilerParams(
+            collective_id=0, has_side_effects=True, vmem_limit_bytes=62 * 1024 * 1024
+        ),
+    )(
+        frames.reshape(steps, rows, width),
+        cotangent.reshape(steps, rows, width),
+        pad,
+        w_in[0],
+        w_out[0],
+        gain_pre,
+        gain_mid,
+        w_depth[0],
+    )
+    return (
+        ig.reshape(1, micro_count, 1, length, width),
+        (scale * total[:, : 2 * width].astype(f32))[None],
+        (scale * total[:, 2 * width :].astype(f32))[None],
+        (scale * small[0])[None],
+        (scale * small[1])[None],
+        (scale * small[8 : 8 + kernel])[None],
+    )
+
+
 def solution(mesh):
     in_specs = (
         P(None, ("fsdp", "batch"), None, None),
@@ -317,4 +908,6 @@
         P("section", None),
         P("section", None, None),
     )
-    return jax.shard_map(local, mesh=mesh, in_specs=in_specs, out_specs=out_specs, check_vma=False)
+    paired = mesh.shape["fsdp"] == 2 and mesh.shape["batch"] == 4
+    body = fused if paired else local
+    return jax.shard_map(body, mesh=mesh, in_specs=in_specs, out_specs=out_specs, check_vma=False)

time: 1150 us -> 414 us (0.36)
  waiting for transfers between devices: 806 us -> 0 us
  Pallas kernels: 0 us -> 394 us
  matrix products: 94.2 us -> 0 us
  local copies, waits for them, and re-layouts: 63.8 us -> 4.18 us
  other arithmetic: 71.9 us -> 14.6 us
  starting transfers between devices: 50.9 us -> 0 us
  blocking collectives: 36.5 us -> 0 us
  between operations: 14.9 us -> 0.67 us
    pallas_call x0 -> x1, Pallas kernels: none -> 394 us  [fused(): pl.pallas_call(functools.partial(pipeline_kernel, (steps, group, length,...]
    psum x2 -> x0, waiting for transfers between devices: 284 us -> none  [the longest x1 248 us: local(): lax.psum(shares[0].astype(jnp.bfloat16), 'batch').astype(jnp.float32)]
    all_gather x2 -> x0, waiting for transfers between devices: 186 us -> none  [the longest x1 120 us: local(): lax.all_gather(w_in[0], 'fsdp', axis=0, tiled=True)]
    ppermute x12 -> x0, waiting for transfers between devices: 171 us -> none  [from_behind(): return lax.ppermute(x, axis, pairs)]
    reduce_scatter x2 -> x0, waiting for transfers between devices: 164 us -> none  [the longest x1 113 us: local(): lax.psum_scatter(rounded_in.astype(jnp.bfloat16), 'fsdp', scatter_dimensi...]
    dot_general x18 -> x0, matrix products: 94.2 us -> none  [the longest x8 43.3 us: project_back(): lax.dot_general(left.reshape(batch_rows * length, inner), right, (((1,),...]
    ppermute x12 -> x0, starting transfers between devices: 50.7 us -> none  [from_behind(): return lax.ppermute(x, axis, pairs)]
    psum x1 -> x0, blocking collectives: 36.5 us -> none  [local(): lax.psum((small_sums[0], small_sums[1], small_sums[2]), ('fsdp', 'batch'))]
  transfers between devices with their start and end apart: 18 -> 0, of which waited for: 18 -> 0; matrix products, arithmetic and copies ran while one was open for 1% -> 0% of each run, Pallas kernels for 0% -> 0%
where the time goes in v1:
time: 414 us; the launch traced here: 413 us
  Pallas kernels  394 us (95%)
  other arithmetic  14.6 us (4%)
  local copies, waits for them, and re-layouts  4.18 us (1%)
    pallas_call x1, Pallas kernels, fused(): pl.pallas_call(functools.partial(pipeline_kernel, (steps, group, length,...  394 us

profile of v1, /device:TPU:0, one launch (start us, length us, event | category | flops | bytes accessed | tf_op | source)
XLA Modules:
  0.0 413.4 jit_solution(14522414653553500798)
XLA Ops:
  0.6 0.5 broadcast.28
  1.1 1.3 reduce.3
  2.5 0.1 lt.31
  2.5 0.1 lt.32
  2.6 0.1 lt.29
  2.7 0.1 lt.35
  2.8 0.7 compare_convert_fusion.pad
  3.6 1.6 copy.25
  5.2 393.9 %shard_map.127 = (bf16[2,96,1536]{2,1,0:T(8,128)(2,1)}, bf16[768,4608]{1,0:T(8,128)(2,1)}, f32[40,1536]{1,0:T(8,128)}) custom-call(bf16[2,96,1536]{2,1,0:T(8,128)(2,1)} %bitcast.22, bf16[2,96,1536]{2,1,0:T(8,128)(2,1)} %bitcast.23, f32[2,96,1]{2,1,0:T(8,128)} %compare_convert_fusion.pad, bf16[768,3072]{1,0:T(8,128)(2,1)} %bitcast.19, ...), custom_call_target="tpu_custom_call" | custom-call | tf_op jit(solution)/shard_map/pallas_call | solution.py:823
  399.1 0.0 copy-start
  399.1 1.6 slice_multiply_fusion
  400.7 1.4 multiply_bitcast_fusion.2
  402.0 0.9 copy.22
  402.9 4.5 %multiply_bitcast_fusion.1 = f32[1,768,1536]{2,1,0:T(8,128)} fusion(bf16[768,4608]{1,0:T(8,128)(2,1)} %get-tuple-element.10), kind=kLoop, calls=%fused_computation.1 | loop fusion | flops 2359296 | bytes 7077888 | tf_op jit(solution)/shard_map/broadcast_in_dim | solution.py:885
  407.4 0.0 copy-done
  407.4 0.0 copy-start.1
  407.4 5.1 %multiply_bitcast_fusion = f32[1,768,3072]{2,1,0:T(8,128)} fusion(bf16[768,4608]{1,0:T(8,128)(2,1)S(1)} %copy-done), kind=kLoop, calls=%fused_computation | loop fusion | flops 4718592 | bytes 14155776 | tf_op jit(solution)/shard_map/broadcast_in_dim | solution.py:884
  412.5 0.0 copy-done.1
  412.5 0.8 copy.27
  (1 shorter events, 0.0 us)
Async XLA Ops:
  399.1 8.4 %copy-start = (bf16[768,4608]{1,0:T(8,128)(2,1)S(1)}, bf16[768,4608]{1,0:T(8,128)(2,1)}, u32[]{:S(2)}) copy-start(bf16[768,4608]{1,0:T(8,128)(2,1)} %get-tuple-element.10) | copy-start | bytes 21233668
  407.4 5.1 %copy-start.1 = (bf16[2,96,1536]{2,1,0:T(8,128)(2,1)S(1)}, bf16[2,96,1536]{2,1,0:T(8,128)(2,1)}, u32[]{:S(2)}) copy-start(bf16[2,96,1536]{2,1,0:T(8,128)(2,1)} %get-tuple-element.9) | copy-start | bytes 1769476

commit v2 on v1

--- a/solution.py
+++ b/solution.py
@@ -305,6 +305,9 @@
 TILE = 256
 LANES = 128
 EDGE = 16
+IN_PIECES = 8
+OUT_PIECES = 4
+IN_FLIGHT = 3
 
 
 def pipeline_kernel(
@@ -341,6 +344,7 @@
     right,
     part,
     arrived,
+    conv_grad,
     small,
     small_y,
     small_sum,
@@ -351,6 +355,7 @@
     w_zs,
     w_zr,
     w_loc,
+    turn,
     f_s,
     f_r,
     b_s,
@@ -413,13 +418,8 @@
         pl.semaphore_signal(barrier, inc=1, device_id=where, device_id_type=pl.DeviceIdType.MESH)
     pl.semaphore_wait(barrier, 5)
 
-    pieces = []
-    in_rows, out_rows = half // 8, half // 4
-    for i in range(6):
-        if i < 4:
-            pieces.append((w_in, win, in_rows, (2 * i, 2 * i)))
-        else:
-            pieces.append((w_out, wout, out_rows, (2 * (i - 4), 2 * (i - 4))))
+    pieces = [(w_in, win, half // 16, 2 * i) for i in range(IN_PIECES)]
+    pieces += [(w_out, wout, half // 8, 2 * i) for i in range(OUT_PIECES)]
 
     def span(size, first, which, owner=None):
         begin = (first + which) * size
@@ -428,7 +428,7 @@
         return pl.ds(pl.multiple_of(begin, 16), size)
 
     def over_y(i):
-        src, dst, size, (first, _) = pieces[i]
+        src, dst, size, first = pieces[i]
         return remote(
             src.at[span(size, first, parity)],
             dst.at[span(size, first, parity, fs)],
@@ -438,12 +438,10 @@
         )
 
     def over_z(i):
-        _, dst, size, (first, _) = pieces[i]
+        _, dst, size, first = pieces[i]
         block = dst.at[span(size, first, parity, other)]
         return remote(block, block, w_zs.at[i], w_zr.at[i], batch=mate)
 
-    for i in range(6):
-        over_y(i).start()
     own = pl.ds(pl.multiple_of(fs * half, 16), half)
     own_in = pltpu.make_async_copy(w_in, win.at[own], w_loc.at[0])
     own_out = pltpu.make_async_copy(w_out, wout.at[own], w_loc.at[1])
@@ -455,13 +453,49 @@
     tg[...] = jnp.zeros_like(tg)
     small[...] = jnp.zeros_like(small)
 
-    for i in range(6):
+    all_pieces = IN_PIECES + OUT_PIECES
+    second_of_pair = lax.rem(sec, 2) == 1
+
+    @pl.when(second_of_pair)
+    def _():
+        pl.semaphore_wait(turn, 1)
+
+    for i in range(IN_FLIGHT):
+        over_y(i).start()
+
+    def pass_on(i):
         over_y(i).wait_recv()
         over_z(i).start()
+        if i + IN_FLIGHT < all_pieces:
+            over_y(i).wait_send()
+            over_y(i + IN_FLIGHT).start()
+
+    for i in range(IN_PIECES):
+        pass_on(i)
     own_in.wait()
-    own_out.wait()
-    for i in range(6):
+    for i in range(IN_PIECES):
         over_z(i).wait_recv()
+
+    def rest_of_weights():
+        for i in range(IN_PIECES, all_pieces):
+            pass_on(i)
+
+        @pl.when(jnp.logical_not(second_of_pair))
+        def _():
+            pl.semaphore_signal(
+                turn,
+                inc=1,
+                device_id={"section": sec + 1},
+                device_id_type=pl.DeviceIdType.MESH,
+            )
+
+        own_out.wait()
+        for i in range(IN_PIECES, all_pieces):
+            over_z(i).wait_recv()
+
+    @pl.when(sec > 0)
+    def _():
+        rest_of_weights()
 
     mine = pl.ds(pl.multiple_of(fs * half, LANES), half)
     theirs = pl.ds(pl.multiple_of(other * half, LANES), half)
@@ -553,6 +587,10 @@
         send_sw(s).start()
         ls[s] = sw[s, :, mine]
 
+        @pl.when((sec == 0) & (s == 0))
+        def _():
+            rest_of_weights()
+
         @pl.when(sec < sections - 1)
         def _():
             def second(j, carry):
@@ -605,17 +643,11 @@
             cols = pl.ds(pl.multiple_of(j * LANES, LANES), LANES)
             gate_cols = pl.ds(pl.multiple_of(width + j * LANES, LANES), LANES)
             cg_all = (mid[:, cols] - s1 - nmid[s, :, cols] * s2) * inv_mid[s]
+            conv_grad[:, cols] = cg_all
             for m in range(group):
                 span_m = slice(m * length, (m + 1) * length)
                 cg = cg_all[span_m]
                 cpad[m, EDGE : EDGE + length, :] = cg
-                for b in range(8):
-                    rolled = gpad[s * group + m, b : b + length + 24, cols]
-                    for a in range(4):
-                        k = 8 * a + b - 1
-                        if 0 <= k < kernel:
-                            term = cg * rolled[8 * a : 8 * a + length]
-                            tg[k, :, cols] += jnp.sum(term.reshape(length // 8, 8, LANES), axis=0)
                 acc = jnp.zeros((length, LANES), f32)
                 for b in range(8):
                     rolled = cpad[m, b : b + length + 24, :]
@@ -657,6 +689,20 @@
         def _():
             send_backward(s).start()
 
+        def fourth(j, carry):
+            cols = pl.ds(pl.multiple_of(j * LANES, LANES), LANES)
+            for m in range(group):
+                cg = conv_grad[m * length : (m + 1) * length, cols]
+                for b in range(8):
+                    rolled = gpad[s * group + m, b : b + length + 24, cols]
+                    for a in range(4):
+                        k = 8 * a + b - 1
+                        if 0 <= k < kernel:
+                            term = cg * rolled[8 * a : 8 * a + length]
+                            tg[k, :, cols] += jnp.sum(term.reshape(length // 8, 8, LANES), axis=0)
+            return carry
+
+        lax.fori_loop(0, width // LANES, fourth, 0)
         return carry
 
     lax.fori_loop(0, steps, backward, 0)
@@ -665,62 +711,100 @@
     swap = remote(small, small_y, sy_s, sy_r, fsdp=other)
     swap.start()
 
-    def arrivals(s, carry):
-        send_proj(s).wait_recv()
+    parts = 6 * tiles
+    depth = half // 2
+
+    def place(p):
+        at = lax.rem(p // 2 + 2 * tiles, 3 * tiles)
+        return pl.ds(pl.multiple_of(lax.rem(p, 2) * depth, 16), depth), tile(at)
+
+    def to_inner(p):
+        where = place(p)
+        return remote(part.at[where], arrived.at[where], a_s.at[p], a_r.at[p], batch=inner)
+
+    def across(p):
+        where = place(p)
+        return remote(part.at[where], total.at[where], c_s.at[p], c_r.at[p], batch=opposite)
+
+    def to_outer(p):
+        where = place(p)
+        return remote(total.at[where], total.at[where], t_s.at[p], t_r.at[p], batch=outer)
+
+    small_to_inner = remote(small_sum, small_a, a_s.at[parts], a_r.at[parts], batch=inner)
+    small_across = remote(small_sum, small_b, c_s.at[parts], c_r.at[parts], batch=opposite)
+    small_to_outer = remote(small_total, small_total, t_s.at[parts], t_r.at[parts], batch=outer)
+
+    tn = (((0,), (0,)), ((), ()))
+
+    def finish(p):
+        where = place(p)
+        across(p).wait_recv()
+        across(p).wait_send()
+        total[where] = (part[where].astype(f32) + total[where].astype(f32)).astype(bf16)
+        to_outer(p).start()
+
+    def terms(left_ref, first_tile, count):
+        def one(order, carry):
+            cols = tile(lax.rem(order + 2 * tiles, 3 * tiles))
+            left = left_ref[...].reshape(2 * steps * rows, half)
+            block = right[:, :, cols].reshape(2 * steps * rows, TILE)
+            part[:, cols] = lax.dot_general(
+                left, block, tn, preferred_element_type=f32
+            ).astype(bf16)
+
+            @pl.when(edge)
+            def _():
+                def send(p, carry):
+                    @pl.when(p >= IN_FLIGHT)
+                    def _():
+                        to_inner(p - IN_FLIGHT).wait_send()
+
+                    to_inner(p).start()
+                    return carry
+
+                lax.fori_loop(2 * order, 2 * order + 2, send, 0)
+
+            @pl.when(jnp.logical_not(edge))
+            def _():
+                def meet(p, carry):
+                    where = place(p)
+                    to_inner(p).wait_recv()
+                    part[where] = (
+                        part[where].astype(f32) + arrived[where].astype(f32)
+                    ).astype(bf16)
+                    across(p).start()
+
+                    @pl.when(p > 0)
+                    def _():
+                        finish(p - 1)
+
+                    return carry
+
+                lax.fori_loop(2 * order, 2 * order + 2, meet, 0)
+
+            return carry
+
+        lax.fori_loop(first_tile, first_tile + count, one, 0)
+
+    def arrivals_out(s, carry):
         send_sw(s).wait_recv()
         send_up(s).wait_recv()
+        return carry
+
+    def arrivals_in(s, carry):
+        send_proj(s).wait_recv()
         send_grad(s).wait_recv()
         return carry
 
-    lax.fori_loop(0, steps, arrivals, 0)
+    lax.fori_loop(0, steps, arrivals_out, 0)
+    terms(ls, 0, tiles)
+    lax.fori_loop(0, steps, arrivals_in, 0)
     swap.wait_recv()
     small_sum[...] = small[...] + small_y[...]
-
-    chunks = 3 * tiles
-
-    def chunk_to_inner(c):
-        return remote(
-            part.at[:, tile(c)], arrived.at[:, tile(c)], a_s.at[c], a_r.at[c], batch=inner
-        )
-
-    def chunk_across(c):
-        return remote(
-            part.at[:, tile(c)], total.at[:, tile(c)], c_s.at[c], c_r.at[c], batch=opposite
-        )
-
-    def chunk_to_outer(c):
-        return remote(
-            total.at[:, tile(c)], total.at[:, tile(c)], t_s.at[c], t_r.at[c], batch=outer
-        )
-
-    small_to_inner = remote(small_sum, small_a, a_s.at[chunks], a_r.at[chunks], batch=inner)
-    small_across = remote(small_sum, small_b, c_s.at[chunks], c_r.at[chunks], batch=opposite)
-    small_to_outer = remote(small_total, small_total, t_s.at[chunks], t_r.at[chunks], batch=outer)
-
-    tn = (((0,), (0,)), ((), ()))
-
-    def terms(left_ref, first_chunk, count):
-        def one(c, carry):
-            left = left_ref[...].reshape(2 * steps * rows, half)
-            block = right[:, :, tile(c)].reshape(2 * steps * rows, TILE)
-            part[:, tile(c)] = lax.dot_general(
-                left, block, tn, preferred_element_type=f32
-            ).astype(bf16)
-
-            @pl.when(edge)
-            def _():
-                chunk_to_inner(c).start()
-
-            return carry
-
-        lax.fori_loop(first_chunk, first_chunk + count, one, 0)
 
     @pl.when(edge)
     def _():
         small_to_inner.start()
-
-    terms(lp, 0, 2 * tiles)
-    terms(ls, 2 * tiles, tiles)
 
     @pl.when(jnp.logical_not(edge))
     def _():
@@ -728,54 +812,41 @@
         small_sum[...] = small_sum[...] + small_a[...]
         small_across.start()
 
-        def finish(c):
-            chunk_across(c).wait_recv()
-            chunk_across(c).wait_send()
-            total[:, tile(c)] = (
-                part[:, tile(c)].astype(f32) + total[:, tile(c)].astype(f32)
-            ).astype(bf16)
-            chunk_to_outer(c).start()
-
-        def meet(c, carry):
-            chunk_to_inner(c).wait_recv()
-            part[:, tile(c)] = (
-                part[:, tile(c)].astype(f32) + arrived[:, tile(c)].astype(f32)
-            ).astype(bf16)
-            chunk_across(c).start()
-
-            @pl.when(c > 0)
-            def _():
-                finish(c - 1)
-
-            return carry
-
-        lax.fori_loop(0, chunks, meet, 0)
-        finish(chunks - 1)
+    terms(lp, tiles, 2 * tiles)
+
+    @pl.when(jnp.logical_not(edge))
+    def _():
         small_across.wait_recv()
         small_across.wait_send()
         small_total[...] = small_sum[...] + small_b[...]
         small_to_outer.start()
-
-        def sent(c, carry):
-            chunk_to_outer(c).wait_send()
+        finish(parts - 1)
+
+        def sent(p, carry):
+            to_outer(p).wait_send()
             return carry
 
-        lax.fori_loop(0, chunks, sent, 0)
+        lax.fori_loop(0, parts, sent, 0)
         small_to_outer.wait_send()
 
     @pl.when(edge)
     def _():
-        def done(c, carry):
-            chunk_to_inner(c).wait_send()
-            chunk_to_outer(c).wait_recv()
+        def left_over(p, carry):
+            to_inner(p).wait_send()
             return carry
 
-        lax.fori_loop(0, chunks, done, 0)
+        def done(p, carry):
+            to_outer(p).wait_recv()
+            return carry
+
+        lax.fori_loop(parts - IN_FLIGHT, parts, left_over, 0)
+        lax.fori_loop(0, parts, done, 0)
         small_to_inner.wait_send()
         small_to_outer.wait_recv()
 
-    for i in range(6):
-        over_y(i).wait_send()
+    for i in range(all_pieces):
+        if i + IN_FLIGHT >= all_pieces:
+            over_y(i).wait_send()
         over_z(i).wait_send()
     swap.wait_send()
 
@@ -809,7 +880,7 @@
     positions = jnp.arange(length, dtype=jnp.int32)
     pad = (positions[None, :] < lengths).astype(jnp.float32).reshape(steps, rows, 1)
     f32, bf16 = jnp.float32, jnp.bfloat16
-    chunks = 3 * (width // TILE)
+    parts = 6 * (width // TILE)
     small_rows = 8 + -(-kernel // 8) * 8
     vmem = pl.BlockSpec(memory_space=pltpu.VMEM)
     hbm = pl.BlockSpec(memory_space=pl.ANY)
@@ -851,20 +922,19 @@
             buf(2 * steps, rows, 3 * width, dtype=bf16),
             buf(half, 3 * width, dtype=bf16),
             buf(half, 3 * width, dtype=bf16),
+            buf(rows, width),
             buf(small_rows, width),
             buf(small_rows, width),
             buf(small_rows, width),
             buf(small_rows, width),
             buf(small_rows, width),
-            sem(6),
-            sem(6),
-            sem(6),
-            sem(6),
+            *[sem(IN_PIECES + OUT_PIECES) for _ in range(4)],
             sem(2),
+            pltpu.SemaphoreType.REGULAR,
             *[sem(steps) for _ in range(12)],
             pltpu.SemaphoreType.DMA,
             pltpu.SemaphoreType.DMA,
-            *[sem(chunks + 1) for _ in range(6)],
+            *[sem(parts + 1) for _ in range(6)],
         ],
         compiler_params=pltpu.CompilerParams(
             collective_id=0, has_side_effects=True, vmem_limit_bytes=62 * 1024 * 1024

time: 414 us -> 387 us (0.935)
  Pallas kernels: 394 us -> 368 us
    pallas_call x1, Pallas kernels: 394 us -> 368 us  [fused(): pl.pallas_call(functools.partial(pipeline_kernel, (steps, group, length,...]
where the time goes in v2:
time: 387 us
  Pallas kernels  368 us (95%)
  other arithmetic  14.6 us (4%)
  local copies, waits for them, and re-layouts  4.18 us (1%)
    pallas_call x1, Pallas kernels, fused(): pl.pallas_call(functools.partial(pipeline_kernel, (steps, group, length,...  368 us

profile of v2, /device:TPU:0, one launch (start us, length us, event | category | flops | bytes accessed | tf_op | source)
XLA Modules:
  0.0 387.1 jit_solution(1293974011389160215)
XLA Ops:
  0.6 0.5 broadcast.28
  1.1 1.3 reduce.3
  2.5 0.1 lt.31
  2.5 0.1 lt.32
  2.6 0.1 lt.29
  2.7 0.1 lt.35
  2.8 0.7 compare_convert_fusion.pad
  3.6 1.6 copy.25
  5.2 367.7 %shard_map.127 = (bf16[2,96,1536]{2,1,0:T(8,128)(2,1)}, bf16[768,4608]{1,0:T(8,128)(2,1)}, f32[40,1536]{1,0:T(8,128)}) custom-call(bf16[2,96,1536]{2,1,0:T(8,128)(2,1)} %bitcast.22, bf16[2,96,1536]{2,1,0:T(8,128)(2,1)} %bitcast.23, f32[2,96,1]{2,1,0:T(8,128)} %compare_convert_fusion.pad, bf16[768,3072]{1,0:T(8,128)(2,1)} %bitcast.19, ...), custom_call_target="tpu_custom_call" | custom-call | tf_op jit(solution)/shard_map/pallas_call | solution.py:894
  372.9 0.0 copy-start
  372.9 1.6 slice_multiply_fusion
  374.5 1.4 multiply_bitcast_fusion.2
  375.8 0.9 copy.22
  376.7 4.5 %multiply_bitcast_fusion.1 = f32[1,768,1536]{2,1,0:T(8,128)} fusion(bf16[768,4608]{1,0:T(8,128)(2,1)} %get-tuple-element.10), kind=kLoop, calls=%fused_computation.1 | loop fusion | flops 2359296 | bytes 7077888 | tf_op jit(solution)/shard_map/broadcast_in_dim | solution.py:955
  381.2 0.0 copy-done
  381.2 0.0 copy-start.1
  381.2 5.1 %multiply_bitcast_fusion = f32[1,768,3072]{2,1,0:T(8,128)} fusion(bf16[768,4608]{1,0:T(8,128)(2,1)S(1)} %copy-done), kind=kLoop, calls=%fused_computation | loop fusion | flops 4718592 | bytes 14155776 | tf_op jit(solution)/shard_map/broadcast_in_dim | solution.py:954
  386.3 0.0 copy-done.1
  386.3 0.8 copy.27
  (1 shorter events, 0.0 us)
Async XLA Ops:
  372.9 8.4 %copy-start = (bf16[768,4608]{1,0:T(8,128)(2,1)S(1)}, bf16[768,4608]{1,0:T(8,128)(2,1)}, u32[]{:S(2)}) copy-start(bf16[768,4608]{1,0:T(8,128)(2,1)} %get-tuple-element.10) | copy-start | bytes 21233668
  381.2 5.1 %copy-start.1 = (bf16[2,96,1536]{2,1,0:T(8,128)(2,1)S(1)}, bf16[2,96,1536]{2,1,0:T(8,128)(2,1)}, u32[]{:S(2)}) copy-start(bf16[2,96,1536]{2,1,0:T(8,128)(2,1)} %get-tuple-element.9) | copy-start | bytes 1769476

commit v3 on v2

--- a/solution.py
+++ b/solution.py
@@ -9,7 +9,7 @@
 from jax.sharding import PartitionSpec as P
 
 epsilon = 1e-05
-GROUP = 2
+GROUP = 1
 
 
 def from_behind(x, axis, by):
@@ -314,7 +314,7 @@
     dims,
     frames,
     cotangent,
-    pad,
+    lengths,
     w_in,
     w_out,
     gain_pre,
@@ -345,6 +345,7 @@
     part,
     arrived,
     conv_grad,
+    pad,
     small,
     small_y,
     small_sum,
@@ -452,6 +453,12 @@
     cpad[...] = jnp.zeros_like(cpad)
     tg[...] = jnp.zeros_like(tg)
     small[...] = jnp.zeros_like(small)
+    frame = lax.broadcasted_iota(jnp.int32, (length, 1), 0)
+    for m in range(steps * group):
+        first_row = (m % group) * length
+        pad[m // group, first_row : first_row + length] = jnp.where(
+            frame < lengths[m, 0], 1.0, 0.0
+        ).astype(f32)
 
     all_pieces = IN_PIECES + OUT_PIECES
     second_of_pair = lax.rem(sec, 2) == 1
@@ -493,7 +500,7 @@
         for i in range(IN_PIECES, all_pieces):
             over_z(i).wait_recv()
 
-    @pl.when(sec > 0)
+    @pl.when(sec > 1)
     def _():
         rest_of_weights()
 
@@ -587,7 +594,7 @@
         send_sw(s).start()
         ls[s] = sw[s, :, mine]
 
-        @pl.when((sec == 0) & (s == 0))
+        @pl.when((sec <= 1) & (s == 0))
         def _():
             rest_of_weights()
 
@@ -877,13 +884,12 @@
     rows = group * length
     half = w_in.shape[1]
     scale = 1.0 / math.sqrt(micro_count * length * lax.axis_size("fsdp") * lax.axis_size("batch"))
-    positions = jnp.arange(length, dtype=jnp.int32)
-    pad = (positions[None, :] < lengths).astype(jnp.float32).reshape(steps, rows, 1)
     f32, bf16 = jnp.float32, jnp.bfloat16
     parts = 6 * (width // TILE)
     small_rows = 8 + -(-kernel // 8) * 8
     vmem = pl.BlockSpec(memory_space=pltpu.VMEM)
     hbm = pl.BlockSpec(memory_space=pl.ANY)
+    smem = pl.BlockSpec(memory_space=pltpu.SMEM)
 
     def buf(*shape, dtype=f32):
         return pltpu.VMEM(shape, dtype)
@@ -898,7 +904,7 @@
             jax.ShapeDtypeStruct((half, 3 * width), bf16),
             jax.ShapeDtypeStruct((small_rows, width), f32),
         ),
-        in_specs=[vmem, vmem, vmem, hbm, hbm, vmem, vmem, vmem],
+        in_specs=[vmem, vmem, smem, hbm, hbm, vmem, vmem, vmem],
         out_specs=(vmem, vmem, vmem),
         scratch_shapes=[
             buf(width, 2 * width, dtype=bf16),
@@ -923,6 +929,7 @@
             buf(half, 3 * width, dtype=bf16),
             buf(half, 3 * width, dtype=bf16),
             buf(rows, width),
+            buf(steps, rows, 1),
             buf(small_rows, width),
             buf(small_rows, width),
             buf(small_rows, width),
@@ -942,7 +949,7 @@
     )(
         frames.reshape(steps, rows, width),
         cotangent.reshape(steps, rows, width),
-        pad,
+        lengths,
         w_in[0],
         w_out[0],
         gain_pre,

time: 387 us -> 400 us (1.034)
  Pallas kernels: 368 us -> 382 us
    pallas_call x1, Pallas kernels: 368 us -> 382 us  [fused(): pl.pallas_call(functools.partial(pipeline_kernel, (steps, group, length,...]
where the time goes in v3:
time: 400 us
  Pallas kernels  382 us (96%)
  other arithmetic  12.6 us (3%)
  local copies, waits for them, and re-layouts  4.62 us (1%)
    pallas_call x1, Pallas kernels, fused(): pl.pallas_call(functools.partial(pipeline_kernel, (steps, group, length,...  382 us

profile of v3, /device:TPU:0, one launch (start us, length us, event | category | flops | bytes accessed | tf_op | source)
XLA Modules:
  0.0 399.9 jit_solution(17850852371364721834)
XLA Ops:
  0.6 1.3 copy.14.lengths
  1.9 1.6 copy.19
  3.6 382.1 %shard_map.127 = (bf16[4,48,1536]{2,1,0:T(8,128)(2,1)}, bf16[768,4608]{1,0:T(8,128)(2,1)}, f32[40,1536]{1,0:T(8,128)}) custom-call(bf16[4,48,1536]{2,1,0:T(8,128)(2,1)} %bitcast.19, bf16[4,48,1536]{2,1,0:T(8,128)(2,1)} %bitcast.20, s32[4,1]{1,0:T(4,128)} %copy.14.lengths, bf16[768,3072]{1,0:T(8,128)(2,1)} %bitcast.16, bf16[768,1536]{1,0:T(8,128)(2,1)} %bitcast.17, ...), custom_call_target="tpu_custom_call" | custom-call | tf_op jit(solution)/shard_map/pallas_call | solution.py:900
  385.7 0.0 copy-start
  385.7 1.6 slice_multiply_fusion
  387.3 1.4 multiply_bitcast_fusion.2
  388.6 0.9 copy.16
  389.5 4.5 %multiply_bitcast_fusion.1 = f32[1,768,1536]{2,1,0:T(8,128)} fusion(bf16[768,4608]{1,0:T(8,128)(2,1)} %get-tuple-element.10), kind=kLoop, calls=%fused_computation.1 | loop fusion | flops 2359296 | bytes 7077888 | tf_op jit(solution)/shard_map/broadcast_in_dim | solution.py:962
  394.0 0.0 copy-done
  394.0 0.0 copy-start.1
  394.0 5.1 %multiply_bitcast_fusion = f32[1,768,3072]{2,1,0:T(8,128)} fusion(bf16[768,4608]{1,0:T(8,128)(2,1)S(1)} %copy-done), kind=kLoop, calls=%fused_computation | loop fusion | flops 4718592 | bytes 14155776 | tf_op jit(solution)/shard_map/broadcast_in_dim | solution.py:961
  399.1 0.0 copy-done.1
  399.1 0.8 copy.21
Async XLA Ops:
  385.7 8.4 %copy-start = (bf16[768,4608]{1,0:T(8,128)(2,1)S(1)}, bf16[768,4608]{1,0:T(8,128)(2,1)}, u32[]{:S(2)}) copy-start(bf16[768,4608]{1,0:T(8,128)(2,1)} %get-tuple-element.10) | copy-start | bytes 21233668
  394.0 5.1 %copy-start.1 = (bf16[4,48,1536]{2,1,0:T(8,128)(2,1)S(1)}, bf16[4,48,1536]{2,1,0:T(8,128)(2,1)}, u32[]{:S(2)}) copy-start(bf16[4,48,1536]{2,1,0:T(8,128)(2,1)} %get-tuple-element.9) | copy-start | bytes 1769476

commit v4 on v3

--- a/solution.py
+++ b/solution.py
@@ -9,7 +9,7 @@
 from jax.sharding import PartitionSpec as P
 
 epsilon = 1e-05
-GROUP = 1
+GROUP = 2
 
 
 def from_behind(x, axis, by):
@@ -626,9 +626,21 @@
         send_up(s).start()
         zero = jnp.zeros((rows, 1), f32)
 
+        def turned(weights, values):
+            def one(j, carry):
+                span_j = pl.ds(pl.multiple_of(j * half, LANES), half)
+                product = lax.dot_general(
+                    weights[span_j, :], values(), nt, preferred_element_type=f32
+                )
+                mid[:, span_j] = product.T
+                return carry
+
+            lax.fori_loop(0, 2, one, 0)
+
+        turned(wout, lambda: right[s, :, pl.ds(2 * width, width)])
+
         def first(j, sums):
-            up = right[s, :, pl.ds(2 * width, width)]
-            sg = lax.dot_general(up, wout[tile(j), :], nt, preferred_element_type=f32)
+            sg = mid[:, tile(j)]
             nm = nmid[s, :, tile(j)]
             gb = gain_mid[:, tile(j)]
             scaled = nm * gb
@@ -674,9 +686,10 @@
         lax.fori_loop(0, width // LANES, second, 0)
         send_grad(s).start()
 
+        turned(win, lambda: right[s, :, pl.ds(0, 2 * width)])
+
         def third(j, sums):
-            pg = right[s, :, pl.ds(0, 2 * width)]
-            ins = lax.dot_general(pg, win[tile(j), :], nt, preferred_element_type=f32)
+            ins = mid[:, tile(j)]
             nv = nin[s, :, tile(j)]
             small[0:1, tile(j)] += jnp.sum(ins * nv, axis=0, keepdims=True)
             z = ins * gain_pre[:, tile(j)]

time: 400 us -> 382 us (0.955)
  Pallas kernels: 382 us -> 364 us
    pallas_call x1, Pallas kernels: 382 us -> 364 us  [fused(): pl.pallas_call(functools.partial(pipeline_kernel, (steps, group, length,...]
where the time goes in v4:
time: 382 us
  Pallas kernels  364 us (95%)
  other arithmetic  12.6 us (3%)
  local copies, waits for them, and re-layouts  4.62 us (1%)
    pallas_call x1, Pallas kernels, fused(): pl.pallas_call(functools.partial(pipeline_kernel, (steps, group, length,...  364 us

profile of v4, /device:TPU:0, one launch (start us, length us, event | category | flops | bytes accessed | tf_op | source)
XLA Modules:
  0.0 381.9 jit_solution(13340956097902054198)
XLA Ops:
  0.6 1.3 copy.14.lengths
  1.9 1.6 copy.19
  3.6 364.0 %shard_map.127 = (bf16[2,96,1536]{2,1,0:T(8,128)(2,1)}, bf16[768,4608]{1,0:T(8,128)(2,1)}, f32[40,1536]{1,0:T(8,128)}) custom-call(bf16[2,96,1536]{2,1,0:T(8,128)(2,1)} %bitcast.19, bf16[2,96,1536]{2,1,0:T(8,128)(2,1)} %bitcast.20, s32[4,1]{1,0:T(4,128)} %copy.14.lengths, bf16[768,3072]{1,0:T(8,128)(2,1)} %bitcast.16, bf16[768,1536]{1,0:T(8,128)(2,1)} %bitcast.17, ...), custom_call_target="tpu_custom_call" | custom-call | tf_op jit(solution)/shard_map/pallas_call | solution.py:913
  367.6 0.0 copy-start
  367.6 1.6 slice_multiply_fusion
  369.2 1.4 multiply_bitcast_fusion.2
  370.5 0.9 copy.16
  371.4 4.5 %multiply_bitcast_fusion.1 = f32[1,768,1536]{2,1,0:T(8,128)} fusion(bf16[768,4608]{1,0:T(8,128)(2,1)} %get-tuple-element.10), kind=kLoop, calls=%fused_computation.1 | loop fusion | flops 2359296 | bytes 7077888 | tf_op jit(solution)/shard_map/broadcast_in_dim | solution.py:975
  375.9 0.0 copy-done
  375.9 0.0 copy-start.1
  375.9 5.1 %multiply_bitcast_fusion = f32[1,768,3072]{2,1,0:T(8,128)} fusion(bf16[768,4608]{1,0:T(8,128)(2,1)S(1)} %copy-done), kind=kLoop, calls=%fused_computation | loop fusion | flops 4718592 | bytes 14155776 | tf_op jit(solution)/shard_map/broadcast_in_dim | solution.py:974
  381.0 0.0 copy-done.1
  381.0 0.8 copy.21
Async XLA Ops:
  367.6 8.4 %copy-start = (bf16[768,4608]{1,0:T(8,128)(2,1)S(1)}, bf16[768,4608]{1,0:T(8,128)(2,1)}, u32[]{:S(2)}) copy-start(bf16[768,4608]{1,0:T(8,128)(2,1)} %get-tuple-element.10) | copy-start | bytes 21233668
  375.9 5.1 %copy-start.1 = (bf16[2,96,1536]{2,1,0:T(8,128)(2,1)S(1)}, bf16[2,96,1536]{2,1,0:T(8,128)(2,1)}, u32[]{:S(2)}) copy-start(bf16[2,96,1536]{2,1,0:T(8,128)(2,1)} %get-tuple-element.9) | copy-start | bytes 1769476
